TPU v7x, 256 devices: a whole 4x4x8 slice. The times are simulated.
256 devices in a mesh: section: 16 (over z, core), fsdp: 16 (over y, x).
Axes of the slice: x: 4, y: 4, z: 8, core: 2. Of those that a mesh axis runs over, the one named last changes fastest.
Arguments:
- grad: bfloat16 [32, 512, 8192], P('section', 'fsdp'), parts along dimension 0
- left_stat: float32 [512, 512, 512], P(('section', 'fsdp')), parts along dimension 0
- right_stat: float32 [512, 512, 512], P(('section', 'fsdp')), parts along dimension 0
- left_root: bfloat16 [512, 512, 512], P(('section', 'fsdp')), parts along dimension 0
- right_root: bfloat16 [512, 512, 512], P(('section', 'fsdp')), parts along dimension 0
- table: int32 [512], P('section'), parts along dimension 0, may hold values from 0 to 31, each once
Outputs:
- update: bfloat16 [32, 512, 8192], P('section', 'fsdp'), parts along dimension 0
- left_new: float32 [512, 512, 512], P(('section', 'fsdp')), parts along dimension 0
- right_new: float32 [512, 512, 512], P(('section', 'fsdp')), parts along dimension 0
There are 16 independent parts, one for each index of `section`. A program takes and returns all parts, laid end to end along the dimension named above; each array names one. Nothing has to cross between parts.
Inputs may be any that keep to these rules, and one draw needn't show every extreme that they name: `table`: each block number stands in exactly one slot; slot s is kept by fsdp device s // 2.
All inputs are finite; a program needn't handle non-finite values.
Results may differ from a plain program's by a relative error of at most 0.0058.
Values may be sent and summed in bfloat16 or wider, within the bound.
No kernel may reach another device: no remote copies, remote signals or barrier semaphores. Data moves between devices by JAX's collectives and lax.ppermute only.
A program may use at most 64 MiB of HBM per device.

v0:
```python
import jax
import jax.numpy as jnp
from jax import lax
from jax.sharding import PartitionSpec as P

stat_decay = 0.95
epsilon = 1e-06


def precondition(block, left, right, lroot, rroot):
    width = block.shape[1]
    gram_left = jnp.einsum("kij,klj->kil", block, block, preferred_element_type=jnp.float32)
    gram_right = jnp.einsum("kji,kjl->kil", block, block, preferred_element_type=jnp.float32)
    left_out = stat_decay * left + (1.0 - stat_decay) / width * gram_left
    right_out = stat_decay * right + (1.0 - stat_decay) / width * gram_right
    half = jnp.einsum("kij,kjl->kil", lroot, block, preferred_element_type=jnp.float32).astype(
        jnp.bfloat16
    )
    precond = jnp.einsum("kij,kjl->kil", half, rroot, preferred_element_type=jnp.float32).astype(
        jnp.bfloat16
    )
    return (left_out, right_out, precond)


def on_device(grad, left_stat, right_stat, left_root, right_root, table):
    devices = lax.axis_size("fsdp")
    block_rows, row_count, width = grad.shape
    slots, order_bs, _ = left_stat.shape
    columns = width // order_bs
    pieces = grad.reshape(block_rows, row_count, columns, order_bs).transpose(0, 2, 1, 3)
    pieces = pieces.reshape(block_rows * columns, row_count, order_bs)
    chosen = jnp.take(pieces, table, axis=0).reshape(devices, slots, row_count, order_bs)
    outgoing = chosen.transpose(1, 0, 2, 3).reshape(slots, devices * row_count, order_bs)
    owned = lax.all_to_all(outgoing, "fsdp", split_axis=1, concat_axis=1, tiled=True)
    gfloat = grad.astype(jnp.float32)
    gpart = jnp.sum(gfloat * gfloat)
    left_new, right_new, precond = precondition(owned, left_stat, right_stat, left_root, right_root)
    returned = lax.all_to_all(
        precond.reshape(slots, devices, row_count, order_bs),
        "fsdp",
        split_axis=1,
        concat_axis=1,
        tiled=True,
    )
    rfloat = lax.optimization_barrier(returned).astype(jnp.float32)
    gsum, psum = lax.psum((gpart, jnp.sum(rfloat * rfloat)), "fsdp")
    ratio = jnp.sqrt(gsum / (psum + epsilon))
    scaled = (ratio * rfloat).astype(jnp.bfloat16)
    by_slot = scaled.transpose(1, 0, 2, 3).reshape(devices * slots, row_count, order_bs)
    inverse = jnp.argsort(table)
    placed = jnp.take(by_slot, inverse, axis=0)
    update = placed.reshape(block_rows, columns, row_count, order_bs).transpose(0, 2, 1, 3)
    return (update.reshape(block_rows, row_count, width), left_new, right_new)


def solution(mesh):
    return jax.shard_map(
        on_device,
        mesh=mesh,
        in_specs=(
            P("section", "fsdp", None),
            P(("section", "fsdp"), None, None),
            P(("section", "fsdp"), None, None),
            P(("section", "fsdp"), None, None),
            P(("section", "fsdp"), None, None),
            P("section"),
        ),
        out_specs=(
            P("section", "fsdp", None),
            P(("section", "fsdp"), None, None),
            P(("section", "fsdp"), None, None),
        ),
        check_vma=False,
    )
```

profile of v0, /device:TPU:96, one launch (start us, length us, event | category | flops | bytes accessed | tf_op | source)
XLA Modules:
  0.0 105.5 jit_solution(9123319613279073213)
XLA Ops:
  0.6 0.0 copy-start
  0.6 0.8 compare_and_fusion.1
  1.4 0.7 compare_select_fusion.1
  2.1 1.6 %copy.43 = bf16[8,8,16,512]{3,2,1,0:T(8,128)(2,1)S(1)} copy(bf16[8,8,16,512]{3,1,2,0:T(8,128)(2,1)} %bitcast.30) | data formatting | bytes 2097152
  3.6 0.1 bitcast_bitcast_fusion
  3.7 0.6 copy.30
  4.3 0.6 gather_fusion
  4.9 0.2 broadcast_select_fusion.1
  5.1 0.1 copy.31
  5.2 0.0 copy-start.2
  5.2 2.0 %copy.32 = bf16[2,512,512]{2,0,1:T(2,128)(2,1)} copy(bf16[2,512,512]{2,1,0:T(8,128)(2,1)S(1)} %bitcast.31) | data formatting | bytes 2097152 | tf_op jit(solution)/shard_map/reshape | solution.py:33
  7.2 7.0 %all-to-all-start = ((bf16[2,512,512]{2,0,1:T(2,128)(2,1)}), bf16[2,512,512]{2,0,1:T(2,128)(2,1)S(1)}, u32[]{:S(2)}, u32[]{:S(2)}) async-start(bf16[2,512,512]{2,0,1:T(2,128)(2,1)} %copy.32), calls=%async_computation | async-start | bytes 2097152 | tf_op jit(solution)/shard_map/all_to_all | solution.py:34
  14.3 0.0 copy-done.2
  14.3 1.6 %sort.17 = (s32[32]{0:T(128)}, s32[32]{0:T(128)S(1)}) sort(s32[32]{0:T(128)S(1)} %copy-done.2, s32[32]{0:T(128)S(1)} %iota.4), dimensions={0}, to_apply=%region_4.6 | sort | flops 160 | bytes 512 | tf_op jit(solution)/shard_map/jit(argsort)/sort | solution.py:50
  15.9 16.0 %all-to-all-done = bf16[2,512,512]{2,0,1:T(2,128)(2,1)S(1)} async-done(((bf16[2,512,512]{2,0,1:T(2,128)(2,1)}), bf16[2,512,512]{2,0,1:T(2,128)(2,1)S(1)}, u32[]{:S(2)}, u32[]{:S(2)}) %all-to-all-start) | async-done | bytes 1048608 | tf_op jit(solution)/shard_map/all_to_all | solution.py:34
  31.9 1.4 %copy.33 = bf16[2,512,512]{1,2,0:T(8,128)(2,1)S(1)} copy(bf16[2,512,512]{2,0,1:T(2,128)(2,1)S(1)} %all-to-all-done) | data formatting | bytes 2097152 | tf_op jit(solution)/shard_map/all_to_all | solution.py:34
  33.4 0.0 copy-done
  33.4 0.0 copy-start.1
  33.4 3.9 %convolution_convert_fusion = bf16[2,512,512]{2,1,0:T(8,128)(2,1)} fusion(bf16[2,512,512]{2,1,0:T(8,128)(2,1)S(1)} %copy-done, bf16[2,512,512]{1,2,0:T(8,128)(2,1)S(1)} %copy.33, bf16[2,512,512]{2,1,0:T(8,128)(2,1)} %param.11), kind=kOutput, calls=%fused_computation.9 | convolution fusion | flops 1074790400 | bytes 4194304 | tf_op jit(solution)/shard_map/kij,kjl->kil/dot_general | solution.py:19
  37.3 0.0 copy-done.1
  37.3 2.3 %copy.35 = bf16[2,16,32,512]{3,2,0,1:T(8,128)(2,1)} copy(bf16[2,16,32,512]{3,2,1,0:T(8,128)(2,1)} %bitcast.34) | data formatting | bytes 2097152 | tf_op jit(solution)/shard_map/reshape | solution.py:39
  39.6 3.7 %all-to-all-start.1 = ((bf16[2,16,32,512]{3,2,0,1:T(8,128)(2,1)}), bf16[2,16,32,512]{3,2,0,1:T(8,128)(2,1)S(1)}, u32[]{:S(2)}, u32[]{:S(2)}) async-start(bf16[2,16,32,512]{3,2,0,1:T(8,128)(2,1)} %copy.35), calls=%async_computation.1 | async-start | bytes 2097152 | tf_op jit(solution)/shard_map/all_to_all | solution.py:38
  43.3 2.4 %multiply_reduce_fusion = f32[]{:T(128)} fusion(bf16[2,32,8192]{2,1,0:T(8,128)(2,1)} %param.8), kind=kLoop, calls=%fused_computation.8 | loop fusion | flops 1572863 | bytes 1048580 | tf_op jit(solution)/shard_map/reduce_sum | solution.py:36
  45.6 4.0 %multiply_add_fusion = f32[2,512,512]{2,1,0:T(8,128)} fusion(f32[2,512,512]{2,1,0:T(8,128)} %param.10, bf16[2,512,512]{1,2,0:T(8,128)(2,1)} %copy-done.1, bf16[2,512,512]{2,0,1:T(2,128)(2,1)S(1)} %all-to-all-done), kind=kOutput, calls=%fused_computation.6 | convolution fusion | flops 538443776 | bytes 6291456 | tf_op jit(solution)/shard_map/kji,kjl->kil/dot_general | solution.py:13
  49.6 9.9 %all-to-all-done.1 = bf16[2,16,32,512]{3,2,0,1:T(8,128)(2,1)S(1)} async-done(((bf16[2,16,32,512]{3,2,0,1:T(8,128)(2,1)}), bf16[2,16,32,512]{3,2,0,1:T(8,128)(2,1)S(1)}, u32[]{:S(2)}, u32[]{:S(2)}) %all-to-all-start.1) | async-done | bytes 1048608 | tf_op jit(solution)/shard_map/all_to_all | solution.py:38
  59.6 1.2 %fusion = f32[]{:T(128)} fusion(bf16[2,16,32,512]{3,2,0,1:T(8,128)(2,1)S(1)} %all-to-all-done.1), kind=kLoop, calls=%fused_computation.4 | loop fusion | flops 1572863 | bytes 1048580 | tf_op jit(solution)/shard_map/reduce_sum | solution.py:46
  60.8 3.8 %multiply_add_fusion.1 = f32[2,512,512]{2,1,0:T(8,128)} fusion(f32[2,512,512]{2,1,0:T(8,128)} %param.9, bf16[2,512,512]{2,0,1:T(2,128)(2,1)S(1)} %all-to-all-done), kind=kOutput, calls=%fused_computation.7 | convolution fusion | flops 538443776 | bytes 5242880 | tf_op jit(solution)/shard_map/kij,klj->kil/dot_general | solution.py:12
  64.5 37.5 %all-reduce = (f32[]{:T(128)}, f32[]{:T(128)}) all-reduce(f32[]{:T(128)} %multiply_reduce_fusion, f32[]{:T(128)} %fusion), channel_id=1, replica_groups=mesh['section'=16,'fsdp'=16] {'fsdp'}, use_global_device_ids=true, to_apply=%region_1.2 | all-reduce | flops 2 | bytes 16 | tf_op jit(solution)/shard_map/psum | solution.py:46
  103.4 0.2 fusion.1
  103.6 0.6 gather_fusion.1
  104.3 0.2 broadcast_select_fusion
  104.4 1.1 %copy.42 = bf16[2,16,4,8,512]{4,3,1,2,0:T(8,128)(2,1)} copy(bf16[2,16,4,8,512]{4,3,2,1,0:T(8,128)(2,1)S(1)} %bitcast.29) | data formatting | bytes 2097152 | tf_op jit(solution)/shard_map/reshape | solution.py:53
  (5 shorter events, 0.0 us)
Async XLA Ops:
  0.6 32.8 %copy-start = (bf16[2,512,512]{2,1,0:T(8,128)(2,1)S(1)}, bf16[2,512,512]{2,1,0:T(8,128)(2,1)}, u32[]{:S(2)}) copy-start(bf16[2,512,512]{2,1,0:T(8,128)(2,1)} %param.12) | copy-start | bytes 3145732
  5.2 9.1 %copy-start.2 = (s32[32]{0:T(128)S(1)}, s32[32]{0:T(128)}, u32[]{:S(2)}) copy-start(s32[32]{0:T(128)} %param.13) | copy-start | bytes 388
  7.2 24.7 %all-to-all-start = ((bf16[2,512,512]{2,0,1:T(2,128)(2,1)}), bf16[2,512,512]{2,0,1:T(2,128)(2,1)S(1)}, u32[]{:S(2)}, u32[]{:S(2)}) async-start(bf16[2,512,512]{2,0,1:T(2,128)(2,1)} %copy.32), calls=%async_computation | async-start | bytes 2097152 | tf_op jit(solution)/shard_map/all_to_all | solution.py:34
  33.4 3.9 %copy-start.1 = (bf16[2,512,512]{1,2,0:T(8,128)(2,1)}, bf16[2,512,512]{1,2,0:T(8,128)(2,1)S(1)}, u32[]{:S(2)}) copy-start(bf16[2,512,512]{1,2,0:T(8,128)(2,1)S(1)} %copy.33) | copy-start | bytes 3145732
  39.6 20.0 %all-to-all-start.1 = ((bf16[2,16,32,512]{3,2,0,1:T(8,128)(2,1)}), bf16[2,16,32,512]{3,2,0,1:T(8,128)(2,1)S(1)}, u32[]{:S(2)}, u32[]{:S(2)}) async-start(bf16[2,16,32,512]{3,2,0,1:T(8,128)(2,1)} %copy.35), calls=%async_computation.1 | async-start | bytes 2097152 | tf_op jit(solution)/shard_map/all_to_all | solution.py:38
where the time goes:
time: 106 us; the launch traced here: 105 us
  blocking collectives  37.5 us (35%)
  waiting for transfers between devices  25.9 us (24%)
  matrix products  11.6 us (11%)
  starting transfers between devices  10.7 us (10%)
  local copies, waits for them, and re-layouts  10.4 us (10%)
  other arithmetic  7.19 us (7%)
  between operations  2.18 us (2%)
    psum x1, blocking collectives, on_device(): gsum, psum = lax.psum((gpart, jnp.sum(rfloat * rfloat)), 'fsdp')  37.5 us
    all_to_all x1, waiting for transfers between devices, on_device(): lax.all_to_all(outgoing, 'fsdp', split_axis=1, concat_axis=1, tiled=True)  16 us
    all_to_all x1, waiting for transfers between devices, on_device(): lax.all_to_all(precond.reshape(slots, devices, row_count, order_bs), 'fsd...  9.91 us
    all_to_all x1, starting transfers between devices, on_device(): lax.all_to_all(outgoing, 'fsdp', split_axis=1, concat_axis=1, tiled=True)  7.03 us
    dot_general x1, matrix products, precondition(): jnp.einsum('kji,kjl->kil', block, block, preferred_element_type=jnp.float32)  4.01 us
    dot_general x1, matrix products, precondition(): jnp.einsum('kij,kjl->kil', half, rroot, preferred_element_type=jnp.float32)  3.86 us
    dot_general x1, matrix products, precondition(): jnp.einsum('kij,klj->kil', block, block, preferred_element_type=jnp.float32)  3.77 us
    all_to_all x1, starting transfers between devices, on_device(): lax.all_to_all(precond.reshape(slots, devices, row_count, order_bs), 'fsd...  3.66 us
  transfers between devices with their start and end apart: 2, of which 2 were waited for; matrix products, arithmetic and copies ran while one was open for 8% of the time, Pallas kernels for 0%

commit v1 on v0

v1 whole, which is shorter than its diff:
```python
import jax
import jax.numpy as jnp
from jax import lax
from jax.experimental import pallas as pl
from jax.experimental.pallas import tpu as pltpu
from jax.sharding import PartitionSpec as P

stat_decay = 0.95
epsilon = 1e-06

DEVICES = 16
SLOTS = 2
ROWS = 32
BS = 512
COLUMNS = 16
LANES = 128
CHUNKS = BS // LANES
BODY = CHUNKS * SLOTS * ROWS
EXTRA = 16
VMEM_LIMIT = 48 * 1024 * 1024


def place(block):
    row = lax.div(block, COLUMNS)
    column = lax.rem(block, COLUMNS)
    return row, pl.ds(pl.multiple_of(column * BS, BS), BS)


def pack_kernel(table_ref, grad_ref, out_ref):
    for s in range(DEVICES * SLOTS):
        row, columns = place(table_ref[s])
        rows = slice(s % SLOTS * ROWS, (s % SLOTS + 1) * ROWS)
        out_ref[s // SLOTS, rows, :] = grad_ref[row, :, columns]


def pack(table, grad):
    return pl.pallas_call(
        pack_kernel,
        out_shape=jax.ShapeDtypeStruct((DEVICES, SLOTS * ROWS, BS), jnp.bfloat16),
        in_specs=[
            pl.BlockSpec(memory_space=pltpu.SMEM),
            pl.BlockSpec(memory_space=pltpu.VMEM),
        ],
        out_specs=pl.BlockSpec(memory_space=pltpu.VMEM),
        compiler_params=pltpu.CompilerParams(vmem_limit_bytes=VMEM_LIMIT),
        name="pack",
    )(table, grad)


def three_terms(value):
    value = 0.5 * value
    high = value.astype(jnp.bfloat16).astype(jnp.float32)
    rest = value - high
    middle = rest.astype(jnp.bfloat16).astype(jnp.float32)
    return high, middle, rest - middle


def precondition_kernel(owned_ref, lroot_ref, rroot_ref, out_ref):
    gpart = jnp.zeros((1, LANES), jnp.float32)
    ppart = jnp.zeros((1, LANES), jnp.float32)
    for t in range(SLOTS):
        rows = slice(t * ROWS, (t + 1) * ROWS)
        block = owned_ref[:, rows, :].reshape(BS, BS)
        half = jnp.dot(lroot_ref[t], block, preferred_element_type=jnp.float32)
        half = half.astype(jnp.bfloat16)
        precond = jnp.dot(half, rroot_ref[t], preferred_element_type=jnp.float32)
        precond = precond.astype(jnp.bfloat16)
        for q in range(CHUNKS):
            lanes = slice(q * LANES, (q + 1) * LANES)
            piece = precond[:, lanes]
            start = (q * SLOTS + t) * ROWS
            out_ref[:, start : start + ROWS, :] = piece.reshape(DEVICES, ROWS, LANES)
            pfloat = piece.astype(jnp.float32)
            ppart += jnp.sum(pfloat * pfloat, axis=0, keepdims=True)
            gfloat = block[:, lanes].astype(jnp.float32)
            gpart += jnp.sum(gfloat * gfloat, axis=0, keepdims=True)
    index = lax.broadcasted_iota(jnp.int32, (EXTRA, LANES), 0)
    tile = jnp.zeros((EXTRA, LANES), jnp.float32)
    for k, term in enumerate(three_terms(gpart) + three_terms(ppart)):
        tile = jnp.where(index == k, term, tile)
    tile = tile.astype(jnp.bfloat16)
    out_ref[:, BODY:, :] = jnp.broadcast_to(tile[None], (DEVICES, EXTRA, LANES))


def precondition(owned, left_root, right_root):
    return pl.pallas_call(
        precondition_kernel,
        out_shape=jax.ShapeDtypeStruct((DEVICES, BODY + EXTRA, LANES), jnp.bfloat16),
        in_specs=[pl.BlockSpec(memory_space=pltpu.VMEM)] * 3,
        out_specs=pl.BlockSpec(memory_space=pltpu.VMEM),
        compiler_params=pltpu.CompilerParams(vmem_limit_bytes=VMEM_LIMIT),
        cost_estimate=pl.CostEstimate(
            flops=4 * SLOTS * BS**3, bytes_accessed=8 * SLOTS * BS * BS, transcendentals=0
        ),
        name="precondition",
    )(owned, left_root, right_root)


PARTS = 2
PART = BS // PARTS


def statistics_kernel(owned_ref, left_ref, right_ref, left_out_ref, right_out_ref):
    rows = pl.ds(pl.multiple_of(pl.program_id(0) * ROWS, ROWS), ROWS)
    part = pl.program_id(1)
    share = DEVICES // PARTS
    block = owned_ref[:, rows, :].reshape(BS, BS)
    some_rows = owned_ref[pl.ds(part * share, share), rows, :].reshape(PART, BS)
    some_columns = owned_ref[:, rows, pl.ds(pl.multiple_of(part * PART, PART), PART)]
    some_columns = some_columns.reshape(BS, PART)
    weight = (1.0 - stat_decay) / BS
    gram = lax.dot_general(
        some_rows, block, (((1,), (1,)), ((), ())), preferred_element_type=jnp.float32
    )
    left_out_ref[0] = stat_decay * left_ref[0] + weight * gram
    gram = lax.dot_general(
        some_columns, block, (((0,), (0,)), ((), ())), preferred_element_type=jnp.float32
    )
    right_out_ref[0] = stat_decay * right_ref[0] + weight * gram


def statistics(owned, left_stat, right_stat):
    spec = pl.BlockSpec((1, PART, BS), lambda t, i: (t, i, 0))
    return pl.pallas_call(
        statistics_kernel,
        grid=(SLOTS, PARTS),
        out_shape=[jax.ShapeDtypeStruct((SLOTS, BS, BS), jnp.float32)] * 2,
        in_specs=[
            pl.BlockSpec((DEVICES, SLOTS * ROWS, BS), lambda t, i: (0, 0, 0)),
            spec,
            spec,
        ],
        out_specs=[spec, spec],
        compiler_params=pltpu.CompilerParams(vmem_limit_bytes=VMEM_LIMIT),
        cost_estimate=pl.CostEstimate(
            flops=4 * SLOTS * BS**3, bytes_accessed=18 * SLOTS * BS * BS, transcendentals=0
        ),
        name="statistics",
    )(owned, left_stat, right_stat)


def unpack_kernel(table_ref, back_ref, out_ref, scaled_ref, sem):
    extra = jnp.sum(back_ref[:, BODY:, :].astype(jnp.float32), axis=0)
    extra = 2.0 * jnp.sum(extra, axis=1, keepdims=True)
    gsum = extra[0:1] + extra[1:2] + extra[2:3]
    psum = extra[3:4] + extra[4:5] + extra[5:6]
    ratio = jnp.sqrt(gsum / (psum + epsilon))
    for s in range(DEVICES * SLOTS):
        for q in range(CHUNKS):
            start = (q * SLOTS + s % SLOTS) * ROWS
            pfloat = back_ref[s // SLOTS, start : start + ROWS, :].astype(jnp.float32)
            scaled_ref[s, :, q * LANES : (q + 1) * LANES] = (ratio * pfloat).astype(jnp.bfloat16)
        row, columns = place(table_ref[s])
        pltpu.make_async_copy(scaled_ref.at[s], out_ref.at[row, :, columns], sem).start()
    pltpu.make_async_copy(out_ref, out_ref, sem).wait()


def unpack(table, back):
    return pl.pallas_call(
        unpack_kernel,
        out_shape=jax.ShapeDtypeStruct((2, ROWS, COLUMNS * BS), jnp.bfloat16),
        in_specs=[
            pl.BlockSpec(memory_space=pltpu.SMEM),
            pl.BlockSpec(memory_space=pltpu.VMEM),
        ],
        out_specs=pl.BlockSpec(memory_space=pl.ANY),
        scratch_shapes=[
            pltpu.VMEM((DEVICES * SLOTS, ROWS, BS), jnp.bfloat16),
            pltpu.SemaphoreType.DMA,
        ],
        compiler_params=pltpu.CompilerParams(vmem_limit_bytes=VMEM_LIMIT),
        name="unpack",
    )(table, back)


def on_device(grad, left_stat, right_stat, left_root, right_root, table):
    outgoing = pack(table, grad)
    owned = lax.all_to_all(outgoing, "fsdp", split_axis=0, concat_axis=0, tiled=True)
    returning = precondition(owned, left_root, right_root)
    back = lax.all_to_all(returning, "fsdp", split_axis=0, concat_axis=0, tiled=True)
    left_new, right_new = statistics(owned, left_stat, right_stat)
    update = unpack(table, back)
    return (update, left_new, right_new)


def solution(mesh):
    return jax.shard_map(
        on_device,
        mesh=mesh,
        in_specs=(
            P("section", "fsdp", None),
            P(("section", "fsdp"), None, None),
            P(("section", "fsdp"), None, None),
            P(("section", "fsdp"), None, None),
            P(("section", "fsdp"), None, None),
            P("section"),
        ),
        out_specs=(
            P("section", "fsdp", None),
            P(("section", "fsdp"), None, None),
            P(("section", "fsdp"), None, None),
        ),
        check_vma=False,
    )
```

time: 106 us -> 52.2 us (0.49)
  waiting for transfers between devices: 25.9 us -> 10.8 us
  blocking collectives: 37.5 us -> 24 us
  matrix products: 11.6 us -> 0 us
  Pallas kernels: 0 us -> 7.71 us
  other arithmetic: 7.19 us -> 0 us
  starting transfers between devices: 10.7 us -> 3.7 us
  local copies, waits for them, and re-layouts: 10.4 us -> 5.06 us
  between operations: 2.18 us -> 0.67 us
    psum x1 -> x0, blocking collectives: 37.5 us -> none  [on_device(): gsum, psum = lax.psum((gpart, jnp.sum(rfloat * rfloat)), 'fsdp')]
    all_to_all x0 -> x1, blocking collectives: none -> 24 us  [on_device(): lax.all_to_all(outgoing, 'fsdp', split_axis=0, concat_axis=0, tiled=True)]
    all_to_all x2 -> x1, waiting for transfers between devices: 25.9 us -> 10.8 us  [on_device(): lax.all_to_all(returning, 'fsdp', split_axis=0, concat_axis=0, tiled=True)]
    dot_general x3 -> x0, matrix products: 11.6 us -> none  [the longest x1 4.01 us: precondition(): jnp.einsum('kji,kjl->kil', block, block, preferred_element_type=jnp.float32)]
    pallas_call x0 -> x4, Pallas kernels: none -> 7.71 us  [the longest x1 3.11 us: statistics(): pl.pallas_call(statistics_kernel, grid=(SLOTS, PARTS), out_shape=[jax.Sha...]
    all_to_all x2 -> x1, starting transfers between devices: 10.7 us -> 3.7 us  [on_device(): lax.all_to_all(returning, 'fsdp', split_axis=0, concat_axis=0, tiled=True)]
    reshape x3 -> x0, local copies, waits for them, and re-layouts: 5.41 us -> none  [the longest x1 2.3 us: on_device(): precond.reshape(slots, devices, row_count, order_bs)]
    reduce_sum x2 -> x0, other arithmetic: 3.59 us -> none  [the longest x1 2.37 us: on_device(): gpart = jnp.sum(gfloat * gfloat)]
  transfers between devices with their start and end apart: 2 -> 1, of which waited for: 2 -> 1; matrix products, arithmetic and copies ran while one was open for 8% -> 0% of each run, Pallas kernels for 0% -> 6%
where the time goes in v1:
time: 52.2 us; the launch traced here: 51.9 us
  blocking collectives  24 us (46%)
  waiting for transfers between devices  10.8 us (21%)
  Pallas kernels  7.71 us (15%)
  local copies, waits for them, and re-layouts  5.06 us (10%)
  starting transfers between devices  3.7 us (7%)
  between operations  0.67 us (1%)
    all_to_all x1, blocking collectives, on_device(): lax.all_to_all(outgoing, 'fsdp', split_axis=0, concat_axis=0, tiled=True)  24 us
    all_to_all x1, waiting for transfers between devices, on_device(): lax.all_to_all(returning, 'fsdp', split_axis=0, concat_axis=0, tiled=True)  10.8 us
    unnamed x14, local copies, waits for them, and re-layouts  5.06 us
    all_to_all x1, starting transfers between devices, on_device(): lax.all_to_all(returning, 'fsdp', split_axis=0, concat_axis=0, tiled=True)  3.7 us
    pallas_call x1, Pallas kernels, statistics(): pl.pallas_call(statistics_kernel, grid=(SLOTS, PARTS), out_shape=[jax.Sha...  3.11 us
    pallas_call x1, Pallas kernels, precondition(): pl.pallas_call(precondition_kernel, out_shape=jax.ShapeDtypeStruct((DEVIC...  2.28 us
    pallas_call x1, Pallas kernels, unpack(): pl.pallas_call(unpack_kernel, out_shape=jax.ShapeDtypeStruct((2, ROWS, CO...  1.64 us
  transfers between devices with their start and end apart: 1, of which 1 were waited for; matrix products, arithmetic and copies ran while one was open for 0% of the time, Pallas kernels for 6%

profile of v1, /device:TPU:96, one launch (start us, length us, event | category | flops | bytes accessed | tf_op | source)
XLA Modules:
  0.0 51.9 jit_solution(11363449546510751998)
XLA Ops:
  0.6 0.0 copy-start.2
  0.6 1.2 %copy-done.2 = bf16[2,32,8192]{2,1,0:T(8,128)(2,1)S(1)} copy-done((bf16[2,32,8192]{2,1,0:T(8,128)(2,1)S(1)}, bf16[2,32,8192]{2,1,0:T(8,128)(2,1)}, u32[]{:S(2)}) %copy-start.2) | copy-done | bytes 1048600
  1.9 0.0 copy-start.5
  1.9 0.7 %copy-done.5 = s32[32]{0:T(128)S(1)} copy-done((s32[32]{0:T(128)S(1)}, s32[32]{0:T(128)}, u32[]{:S(2)}) %copy-start.5) | copy-done | bytes 152
  2.5 0.0 copy-start.3
  2.5 0.0 copy-start.4
  2.5 0.7 %pack.1 = bf16[16,64,512]{2,1,0:T(8,128)(2,1)S(1)} custom-call(s32[32]{0:T(128)S(1)} %copy-done.5, bf16[2,32,8192]{2,1,0:T(8,128)(2,1)S(1)} %copy-done.2), custom_call_target="tpu_custom_call" | custom-call | tf_op jit(solution)/shard_map/pack/pallas_call | solution.py:37
  3.2 24.0 %all_to_all.10.owned_ref = bf16[16,64,512]{2,1,0:T(8,128)(2,1)S(1)} all-to-all(bf16[16,64,512]{2,1,0:T(8,128)(2,1)S(1)} %pack.1), channel_id=1, replica_groups=mesh['section'=16,'fsdp'=16] {'fsdp'}, dimensions={0} | all-to-all | bytes 2097152 | tf_op jit(solution)/shard_map/all_to_all | solution.py:178
  27.2 0.0 copy-done.3
  27.2 0.0 copy-done.4
  27.2 2.3 %precondition.1 = bf16[16,272,128]{2,1,0:T(8,128)(2,1)} custom-call(bf16[16,64,512]{2,1,0:T(8,128)(2,1)S(1)} %all_to_all.10.owned_ref, bf16[2,512,512]{2,1,0:T(8,128)(2,1)S(1)} %copy-done.3, bf16[2,512,512]{2,1,0:T(8,128)(2,1)S(1)} %copy-done.4), custom_call_target="tpu_custom_call" | custom-call | flops 1073741824 | bytes 4194304 | tf_op jit(solution)/shard_map/precondition/pallas_call | solution.py:86
  29.5 3.7 %all-to-all-start.1 = ((bf16[16,272,128]{2,1,0:T(8,128)(2,1)}), bf16[16,272,128]{2,1,0:T(8,128)(2,1)S(1)}, u32[]{:S(2)}, u32[]{:S(2)}) async-start(bf16[16,272,128]{2,1,0:T(8,128)(2,1)} %precondition.1), calls=%async_computation.1 | async-start | bytes 2228224 | tf_op jit(solution)/shard_map/all_to_all | solution.py:180
  33.2 0.0 copy-start
  33.2 1.6 %copy-done = f32[2,512,512]{2,1,0:T(8,128)S(1)} copy-done((f32[2,512,512]{2,1,0:T(8,128)S(1)}, f32[2,512,512]{2,1,0:T(8,128)}, u32[]{:S(2)}) %copy-start) | copy-done | bytes 2097176
  34.8 0.0 copy-start.1
  34.8 1.6 %copy-done.1 = f32[2,512,512]{2,1,0:T(8,128)S(1)} copy-done((f32[2,512,512]{2,1,0:T(8,128)S(1)}, f32[2,512,512]{2,1,0:T(8,128)}, u32[]{:S(2)}) %copy-start.1) | copy-done | bytes 2097176
  36.4 0.0 copy-start.6
  36.4 3.1 %statistics.1 = (f32[2,512,512]{2,1,0:T(8,128)}, f32[2,512,512]{2,1,0:T(8,128)}) custom-call(bf16[16,64,512]{2,1,0:T(8,128)(2,1)S(1)} %all_to_all.10.owned_ref, f32[2,512,512]{2,1,0:T(8,128)S(1)} %copy-done, f32[2,512,512]{2,1,0:T(8,128)S(1)} %copy-done.1), custom_call_target="tpu_custom_call" | custom-call | flops 1073741824 | bytes 9437184 | tf_op jit(solution)/shard_map/statistics/pallas_call | solution.py:124
  39.5 10.8 %all-to-all-done.1.back_ref = bf16[16,272,128]{2,1,0:T(8,128)(2,1)S(1)} async-done(((bf16[16,272,128]{2,1,0:T(8,128)(2,1)}), bf16[16,272,128]{2,1,0:T(8,128)(2,1)S(1)}, u32[]{:S(2)}, u32[]{:S(2)}) %all-to-all-start.1) | async-done | bytes 1114144 | tf_op jit(solution)/shard_map/all_to_all | solution.py:180
  50.3 0.0 copy-done.6
  50.3 1.6 %unpack.1 = bf16[2,32,8192]{2,1,0:T(8,128)(2,1)} custom-call(s32[32]{0:T(128)S(1)} %copy-done.6, bf16[16,272,128]{2,1,0:T(8,128)(2,1)S(1)} %all-to-all-done.1.back_ref), custom_call_target="tpu_custom_call" | custom-call | tf_op jit(solution)/shard_map/unpack/pallas_call | solution.py:159
Async XLA Ops:
  0.6 1.2 %copy-start.2 = (bf16[2,32,8192]{2,1,0:T(8,128)(2,1)S(1)}, bf16[2,32,8192]{2,1,0:T(8,128)(2,1)}, u32[]{:S(2)}) copy-start(bf16[2,32,8192]{2,1,0:T(8,128)(2,1)} %grad_ref.1) | copy-start | bytes 3145732
  1.9 0.7 %copy-start.5 = (s32[32]{0:T(128)S(1)}, s32[32]{0:T(128)}, u32[]{:S(2)}) copy-start(s32[32]{0:T(128)} %table_ref.3) | copy-start | bytes 388
  2.5 24.7 %copy-start.3 = (bf16[2,512,512]{2,1,0:T(8,128)(2,1)S(1)}, bf16[2,512,512]{2,1,0:T(8,128)(2,1)}, u32[]{:S(2)}) copy-start(bf16[2,512,512]{2,1,0:T(8,128)(2,1)} %lroot_ref.1) | copy-start | bytes 3145732
  2.5 24.7 %copy-start.4 = (bf16[2,512,512]{2,1,0:T(8,128)(2,1)S(1)}, bf16[2,512,512]{2,1,0:T(8,128)(2,1)}, u32[]{:S(2)}) copy-start(bf16[2,512,512]{2,1,0:T(8,128)(2,1)} %rroot_ref.1) | copy-start | bytes 3145732
  29.5 20.8 %all-to-all-start.1 = ((bf16[16,272,128]{2,1,0:T(8,128)(2,1)}), bf16[16,272,128]{2,1,0:T(8,128)(2,1)S(1)}, u32[]{:S(2)}, u32[]{:S(2)}) async-start(bf16[16,272,128]{2,1,0:T(8,128)(2,1)} %precondition.1), calls=%async_computation.1 | async-start | bytes 2228224 | tf_op jit(solution)/shard_map/all_to_all | solution.py:180
  33.2 1.6 %copy-start = (f32[2,512,512]{2,1,0:T(8,128)S(1)}, f32[2,512,512]{2,1,0:T(8,128)}, u32[]{:S(2)}) copy-start(f32[2,512,512]{2,1,0:T(8,128)} %left_ref.1) | copy-start | bytes 6291460
  34.8 1.6 %copy-start.1 = (f32[2,512,512]{2,1,0:T(8,128)S(1)}, f32[2,512,512]{2,1,0:T(8,128)}, u32[]{:S(2)}) copy-start(f32[2,512,512]{2,1,0:T(8,128)} %right_ref.1) | copy-start | bytes 6291460
  36.4 13.9 %copy-start.6 = (s32[32]{0:T(128)S(1)}, s32[32]{0:T(128)}, u32[]{:S(2)}) copy-start(s32[32]{0:T(128)} %table_ref.3) | copy-start | bytes 388

commit v2 on v1

v2 whole, which is shorter than its diff:
```python
import jax
import jax.numpy as jnp
from jax import lax
from jax.experimental import pallas as pl
from jax.experimental.pallas import tpu as pltpu
from jax.sharding import PartitionSpec as P

stat_decay = 0.95
epsilon = 1e-06

DEVICES = 16
SLOTS = 2
ROWS = 32
BS = 512
COLUMNS = 16
LANES = 128
CHUNKS = BS // LANES
BODY = CHUNKS * SLOTS * ROWS
EXTRA = 16
VMEM_LIMIT = 12 * 1024 * 1024
GRAD_PARTS = 4


def place(block):
    row = lax.div(block, COLUMNS)
    column = lax.rem(block, COLUMNS)
    return row, pl.ds(pl.multiple_of(column * BS, BS), BS)


def second_turn():
    return lax.rem(lax.axis_index("section"), 2) == 0


def pack_kernel(
    table_hbm, grad_hbm, right_hbm, out_ref, decayed_hbm,
    table_ref, slot_ref, grad_ref, stat_ref, table_sem, grad_sem, load_sem, store_sem,
):
    table_copy = pltpu.make_async_copy(table_hbm, table_ref, table_sem)
    table_copy.start()
    blocks = 2 * COLUMNS // GRAD_PARTS
    copies = []
    for part in range(GRAD_PARTS):
        row, column = divmod(part * blocks, COLUMNS)
        where = (row, slice(None), pl.ds(column * BS, blocks * BS))
        copies.append(
            pltpu.make_async_copy(grad_hbm.at[where], grad_ref.at[where], grad_sem.at[part])
        )
        copies[-1].start()
    table_copy.wait()
    for s in range(DEVICES * SLOTS):
        slot_ref[table_ref[s]] = s
    for block in range(2 * COLUMNS):
        if block % blocks == 0:
            copies[block // blocks].wait()
        row, column = divmod(block, COLUMNS)
        s = slot_ref[block]
        out_ref[lax.div(s, SLOTS), lax.rem(s, SLOTS)] = grad_ref[
            row, :, column * BS : (column + 1) * BS
        ]

    @pl.when(second_turn())
    def _():
        for t in range(SLOTS):
            load = pltpu.make_async_copy(right_hbm.at[t], stat_ref, load_sem)
            load.start()
            load.wait()
            stat_ref[...] = stat_decay * stat_ref[...]
            store = pltpu.make_async_copy(stat_ref, decayed_hbm.at[t], store_sem)
            store.start()
            store.wait()


def in_hbm(array):
    return pltpu.with_memory_space_constraint(array, pltpu.HBM)


def pack(table, grad, right_stat):
    return pl.pallas_call(
        pack_kernel,
        out_shape=[
            jax.ShapeDtypeStruct((DEVICES, SLOTS, ROWS, BS), jnp.bfloat16),
            pltpu.HBM((SLOTS, BS, BS), jnp.float32),
        ],
        in_specs=[pl.BlockSpec(memory_space=pl.ANY)] * 3,
        out_specs=[
            pl.BlockSpec(memory_space=pltpu.VMEM),
            pl.BlockSpec(memory_space=pl.ANY),
        ],
        scratch_shapes=[
            pltpu.SMEM((DEVICES * SLOTS,), jnp.int32),
            pltpu.SMEM((DEVICES * SLOTS,), jnp.int32),
            pltpu.VMEM((2, ROWS, COLUMNS * BS), jnp.bfloat16),
            pltpu.VMEM((BS, BS), jnp.float32),
            pltpu.SemaphoreType.DMA,
            pltpu.SemaphoreType.DMA((GRAD_PARTS,)),
            pltpu.SemaphoreType.DMA,
            pltpu.SemaphoreType.DMA,
        ],
        compiler_params=pltpu.CompilerParams(vmem_limit_bytes=VMEM_LIMIT),
        name="pack",
    )(*map(in_hbm, (table, grad, right_stat)))


def three_terms(value):
    value = 0.5 * value
    high = value.astype(jnp.bfloat16).astype(jnp.float32)
    rest = value - high
    middle = rest.astype(jnp.bfloat16).astype(jnp.float32)
    return high, middle, rest - middle


def precondition_kernel(owned_ref, lroot_ref, rroot_ref, out_hbm, out_ref, sem):
    gpart = jnp.zeros((1, LANES), jnp.float32)
    ppart = jnp.zeros((1, LANES), jnp.float32)
    copies = []
    for t in range(SLOTS):
        block = owned_ref[:, t].reshape(BS, BS)
        half = jnp.dot(lroot_ref[t], block, preferred_element_type=jnp.float32)
        half = half.astype(jnp.bfloat16)
        precond = jnp.dot(half, rroot_ref[t], preferred_element_type=jnp.float32)
        precond = precond.astype(jnp.bfloat16)
        for q in range(CHUNKS):
            lanes = slice(q * LANES, (q + 1) * LANES)
            piece = precond[:, lanes]
            start = (t * CHUNKS + q) * ROWS
            out_ref[:, start : start + ROWS, :] = piece.reshape(DEVICES, ROWS, LANES)
            pfloat = piece.astype(jnp.float32)
            ppart += jnp.sum(pfloat * pfloat, axis=0, keepdims=True)
            gfloat = block[:, lanes].astype(jnp.float32)
            gpart += jnp.sum(gfloat * gfloat, axis=0, keepdims=True)
        if t == SLOTS - 1:
            index = lax.broadcasted_iota(jnp.int32, (EXTRA, LANES), 0)
            tile = jnp.zeros((EXTRA, LANES), jnp.float32)
            for k, term in enumerate(three_terms(gpart) + three_terms(ppart)):
                tile = jnp.where(index == k, term, tile)
            tile = tile.astype(jnp.bfloat16)
            out_ref[:, BODY:, :] = jnp.broadcast_to(tile[None], (DEVICES, EXTRA, LANES))
        start = t * CHUNKS * ROWS
        rows = pl.ds(start, (CHUNKS * ROWS if t < SLOTS - 1 else BODY + EXTRA - start))
        copies.append(
            pltpu.make_async_copy(out_ref.at[:, rows], out_hbm.at[:, rows], sem.at[t])
        )
        copies[-1].start()
    for copy in copies:
        copy.wait()


def precondition(owned, left_root, right_root):
    shape = (DEVICES, BODY + EXTRA, LANES)
    return pl.pallas_call(
        precondition_kernel,
        out_shape=jax.ShapeDtypeStruct(shape, jnp.bfloat16),
        in_specs=[pl.BlockSpec(memory_space=pltpu.VMEM)] * 3,
        out_specs=pl.BlockSpec(memory_space=pl.ANY),
        scratch_shapes=[
            pltpu.VMEM(shape, jnp.bfloat16),
            pltpu.SemaphoreType.DMA((SLOTS,)),
        ],
        compiler_params=pltpu.CompilerParams(vmem_limit_bytes=VMEM_LIMIT),
        cost_estimate=pl.CostEstimate(
            flops=4 * SLOTS * BS**3, bytes_accessed=8 * SLOTS * BS * BS, transcendentals=0
        ),
        name="precondition",
    )(owned, left_root, right_root)


def statistics_kernel(
    owned_ref, left_hbm, right_hbm, decayed_hbm, left_out, right_out, stat_ref, load_sem, store_sem
):
    second = second_turn()
    loads = {}
    for t in range(SLOTS):
        for side, stat_hbm in enumerate((left_hbm, right_hbm)):
            where, sem = stat_ref.at[side, t], load_sem.at[side, t]
            loads[side, t] = pltpu.make_async_copy(stat_hbm.at[t], where, sem)
            if side == 0:
                loads[side, t].start()
            else:
                early = pltpu.make_async_copy(decayed_hbm.at[t], where, sem)
                pl.when(second)(early.start)
                pl.when(jnp.logical_not(second))(loads[side, t].start)
    decays = stat_decay, jnp.where(second, 1.0, stat_decay).astype(jnp.float32)
    weight = (1.0 - stat_decay) / BS
    stores = []
    for t in range(SLOTS):
        block = owned_ref[:, t].reshape(BS, BS)
        for side, out_hbm in enumerate((left_out, right_out)):
            dims = (((1 - side,), (1 - side,)), ((), ()))
            gram = lax.dot_general(block, block, dims, preferred_element_type=jnp.float32)
            loads[side, t].wait()
            stat_ref[side, t] = decays[side] * stat_ref[side, t] + weight * gram
            stores.append(
                pltpu.make_async_copy(stat_ref.at[side, t], out_hbm.at[t], store_sem.at[side, t])
            )
            stores[-1].start()
    for store in stores:
        store.wait()


def statistics(owned, left_stat, right_stat, decayed):
    return pl.pallas_call(
        statistics_kernel,
        out_shape=[jax.ShapeDtypeStruct((SLOTS, BS, BS), jnp.float32)] * 2,
        in_specs=[pl.BlockSpec(memory_space=pltpu.VMEM)] + [pl.BlockSpec(memory_space=pl.ANY)] * 3,
        out_specs=[pl.BlockSpec(memory_space=pltpu.HBM)] * 2,
        scratch_shapes=[
            pltpu.VMEM((2, SLOTS, BS, BS), jnp.float32),
            pltpu.SemaphoreType.DMA((2, SLOTS)),
            pltpu.SemaphoreType.DMA((2, SLOTS)),
        ],
        compiler_params=pltpu.CompilerParams(vmem_limit_bytes=VMEM_LIMIT),
        cost_estimate=pl.CostEstimate(
            flops=4 * SLOTS * BS**3, bytes_accessed=18 * SLOTS * BS * BS, transcendentals=0
        ),
        name="statistics",
    )(owned, *map(in_hbm, (left_stat, right_stat, decayed)))


def unpack_kernel(table_ref, back_ref, out_ref, scaled_ref, sem):
    extra = jnp.sum(back_ref[:, BODY:, :].astype(jnp.float32), axis=0)
    extra = 2.0 * jnp.sum(extra, axis=1, keepdims=True)
    gsum = extra[0:1] + extra[1:2] + extra[2:3]
    psum = extra[3:4] + extra[4:5] + extra[5:6]
    ratio = jnp.sqrt(gsum / (psum + epsilon))
    for s in range(DEVICES * SLOTS):
        for q in range(CHUNKS):
            start = (s % SLOTS * CHUNKS + q) * ROWS
            pfloat = back_ref[s // SLOTS, start : start + ROWS, :].astype(jnp.float32)
            scaled_ref[s, :, q * LANES : (q + 1) * LANES] = (ratio * pfloat).astype(jnp.bfloat16)
        row, columns = place(table_ref[s])
        pltpu.make_async_copy(scaled_ref.at[s], out_ref.at[row, :, columns], sem).start()
    pltpu.make_async_copy(out_ref, out_ref, sem).wait()


def unpack(table, back):
    return pl.pallas_call(
        unpack_kernel,
        out_shape=jax.ShapeDtypeStruct((2, ROWS, COLUMNS * BS), jnp.bfloat16),
        in_specs=[
            pl.BlockSpec(memory_space=pltpu.SMEM),
            pl.BlockSpec(memory_space=pltpu.VMEM),
        ],
        out_specs=pl.BlockSpec(memory_space=pl.ANY),
        scratch_shapes=[
            pltpu.VMEM((DEVICES * SLOTS, ROWS, BS), jnp.bfloat16),
            pltpu.SemaphoreType.DMA,
        ],
        compiler_params=pltpu.CompilerParams(vmem_limit_bytes=VMEM_LIMIT),
        name="unpack",
    )(table, back)


def on_device(grad, left_stat, right_stat, left_root, right_root, table):
    outgoing, decayed = pack(table, grad, right_stat)
    owned = lax.all_to_all(outgoing, "fsdp", split_axis=0, concat_axis=0, tiled=True)
    returning = precondition(owned, left_root, right_root)
    back = lax.all_to_all(returning, "fsdp", split_axis=0, concat_axis=0, tiled=True)
    left_new, right_new = statistics(owned, left_stat, right_stat, decayed)
    update = unpack(table, back)
    return (update, left_new, right_new)


def solution(mesh):
    return jax.shard_map(
        on_device,
        mesh=mesh,
        in_specs=(
            P("section", "fsdp", None),
            P(("section", "fsdp"), None, None),
            P(("section", "fsdp"), None, None),
            P(("section", "fsdp"), None, None),
            P(("section", "fsdp"), None, None),
            P("section"),
        ),
        out_specs=(
            P("section", "fsdp", None),
            P(("section", "fsdp"), None, None),
            P(("section", "fsdp"), None, None),
        ),
        check_vma=False,
    )
```

time: 52.2 us -> 48.1 us (0.921)
  Pallas kernels: 7.71 us -> 14.4 us
  local copies, waits for them, and re-layouts: 5.06 us -> 0.01 us
  blocking collectives: 24 us -> 19.8 us
  waiting for transfers between devices: 10.8 us -> 9.24 us
    pallas_call x3, Pallas kernels: 6.07 us -> 12.7 us  [the longest x1 6.06 us: pack(): pl.pallas_call(pack_kernel, out_shape=[jax.ShapeDtypeStruct((DEVICES, SLO...]
    unnamed x14 -> x6, local copies, waits for them, and re-layouts: 5.06 us -> 0.01 us
    all_to_all x1, blocking collectives: 24 us -> 19.8 us  [on_device(): lax.all_to_all(outgoing, 'fsdp', split_axis=0, concat_axis=0, tiled=True)]
    all_to_all x1, waiting for transfers between devices: 10.8 us -> 9.24 us  [on_device(): lax.all_to_all(returning, 'fsdp', split_axis=0, concat_axis=0, tiled=True)]
  transfers between devices with their start and end apart: 1 -> 1, of which waited for: 1 -> 1; matrix products, arithmetic and copies ran while one was open for 0% -> 0% of each run, Pallas kernels for 6% -> 9%
where the time goes in v2:
time: 48.1 us; the launch traced here: 47.8 us
  blocking collectives  19.8 us (41%)
  Pallas kernels  14.4 us (30%)
  waiting for transfers between devices  9.24 us (19%)
  starting transfers between devices  3.71 us (8%)
  between operations  0.69 us (1%)
    all_to_all x1, blocking collectives, on_device(): lax.all_to_all(outgoing, 'fsdp', split_axis=0, concat_axis=0, tiled=True)  19.8 us
    all_to_all x1, waiting for transfers between devices, on_device(): lax.all_to_all(returning, 'fsdp', split_axis=0, concat_axis=0, tiled=True)  9.24 us
    pallas_call x1, Pallas kernels, pack(): pl.pallas_call(pack_kernel, out_shape=[jax.ShapeDtypeStruct((DEVICES, SLO...  6.06 us
    pallas_call x1, Pallas kernels, statistics(): pl.pallas_call(statistics_kernel, out_shape=[jax.ShapeDtypeStruct((SLOTS,...  4.5 us
    all_to_all x1, starting transfers between devices, on_device(): lax.all_to_all(returning, 'fsdp', split_axis=0, concat_axis=0, tiled=True)  3.71 us
    pallas_call x1, Pallas kernels, precondition(): pl.pallas_call(precondition_kernel, out_shape=jax.ShapeDtypeStruct(shape,...  2.16 us
    pallas_call x1, Pallas kernels, unpack(): pl.pallas_call(unpack_kernel, out_shape=jax.ShapeDtypeStruct((2, ROWS, CO...  1.64 us
  transfers between devices with their start and end apart: 1, of which 1 were waited for; matrix products, arithmetic and copies ran while one was open for 0% of the time, Pallas kernels for 9%

profile of v2, /device:TPU:96, one launch (start us, length us, event | category | flops | bytes accessed | tf_op | source)
XLA Modules:
  0.0 47.8 jit_solution(7668766066836218331)
XLA Ops:
  0.6 0.0 copy-start.1
  0.6 0.0 copy-start
  0.7 6.1 %pack.1 = (bf16[16,2,32,512]{3,2,1,0:T(8,128)(2,1)S(1)}, f32[2,512,512]{2,1,0:T(8,128)}) custom-call(s32[32]{0:T(128)} %table_ref.1, bf16[2,32,8192]{2,1,0:T(8,128)(2,1)} %grad_hbm.1, f32[2,512,512]{2,1,0:T(8,128)} %right_hbm.3), custom_call_target="tpu_custom_call" | custom-call | tf_op jit(solution)/shard_map/pack/pallas_call | solution.py:78
  6.7 19.8 %all_to_all.10.owned_ref = bf16[16,2,32,512]{3,2,1,0:T(8,128)(2,1)S(1)} all-to-all(bf16[16,2,32,512]{3,2,1,0:T(8,128)(2,1)S(1)} %get-tuple-element.7), channel_id=1, replica_groups=mesh['section'=16,'fsdp'=16] {'fsdp'}, dimensions={0} | all-to-all | bytes 2097152 | tf_op jit(solution)/shard_map/all_to_all | solution.py:255
  26.6 0.0 copy-done.1
  26.6 0.0 copy-done
  26.6 2.2 %precondition.1 = bf16[16,272,128]{2,1,0:T(8,128)(2,1)} custom-call(bf16[16,2,32,512]{3,2,1,0:T(8,128)(2,1)S(1)} %all_to_all.10.owned_ref, bf16[2,512,512]{2,1,0:T(8,128)(2,1)S(1)} %copy-done, bf16[2,512,512]{2,1,0:T(8,128)(2,1)S(1)} %copy-done.1), custom_call_target="tpu_custom_call" | custom-call | flops 1073741824 | bytes 4194304 | tf_op jit(solution)/shard_map/precondition/pallas_call | solution.py:150
  28.7 3.7 %all-to-all-start.1 = ((bf16[16,272,128]{2,1,0:T(8,128)(2,1)}), bf16[16,272,128]{2,1,0:T(8,128)(2,1)S(1)}, u32[]{:S(2)}, u32[]{:S(2)}) async-start(bf16[16,272,128]{2,1,0:T(8,128)(2,1)} %precondition.1), calls=%async_computation.1 | async-start | bytes 2228224 | tf_op jit(solution)/shard_map/all_to_all | solution.py:257
  32.4 0.0 copy-start.2
  32.4 4.5 %statistics.1 = (f32[2,512,512]{2,1,0:T(8,128)}, f32[2,512,512]{2,1,0:T(8,128)}) custom-call(bf16[16,2,32,512]{3,2,1,0:T(8,128)(2,1)S(1)} %all_to_all.10.owned_ref, f32[2,512,512]{2,1,0:T(8,128)} %left_hbm.1, f32[2,512,512]{2,1,0:T(8,128)} %right_hbm.3, f32[2,512,512]{2,1,0:T(8,128)} %get-tuple-element.8.decayed_hbm), custom_call_target="tpu_custom_call" | custom-call | flops 1073741824 | bytes 9437184 | tf_op jit(solution)/shard_map/statistics/pallas_call | solution.py:201
  37.0 9.2 %all-to-all-done.1.back_ref = bf16[16,272,128]{2,1,0:T(8,128)(2,1)S(1)} async-done(((bf16[16,272,128]{2,1,0:T(8,128)(2,1)}), bf16[16,272,128]{2,1,0:T(8,128)(2,1)S(1)}, u32[]{:S(2)}, u32[]{:S(2)}) %all-to-all-start.1) | async-done | bytes 1114144 | tf_op jit(solution)/shard_map/all_to_all | solution.py:257
  46.2 0.0 copy-done.2
  46.2 1.6 %unpack.1 = bf16[2,32,8192]{2,1,0:T(8,128)(2,1)} custom-call(s32[32]{0:T(128)S(1)} %copy-done.2, bf16[16,272,128]{2,1,0:T(8,128)(2,1)S(1)} %all-to-all-done.1.back_ref), custom_call_target="tpu_custom_call" | custom-call | tf_op jit(solution)/shard_map/unpack/pallas_call | solution.py:236
Async XLA Ops:
  0.6 25.9 %copy-start.1 = (bf16[2,512,512]{2,1,0:T(8,128)(2,1)S(1)}, bf16[2,512,512]{2,1,0:T(8,128)(2,1)}, u32[]{:S(2)}) copy-start(bf16[2,512,512]{2,1,0:T(8,128)(2,1)} %rroot_ref.1) | copy-start | bytes 3145732
  0.6 25.9 %copy-start = (bf16[2,512,512]{2,1,0:T(8,128)(2,1)S(1)}, bf16[2,512,512]{2,1,0:T(8,128)(2,1)}, u32[]{:S(2)}) copy-start(bf16[2,512,512]{2,1,0:T(8,128)(2,1)} %lroot_ref.1) | copy-start | bytes 3145732
  28.7 17.5 %all-to-all-start.1 = ((bf16[16,272,128]{2,1,0:T(8,128)(2,1)}), bf16[16,272,128]{2,1,0:T(8,128)(2,1)S(1)}, u32[]{:S(2)}, u32[]{:S(2)}) async-start(bf16[16,272,128]{2,1,0:T(8,128)(2,1)} %precondition.1), calls=%async_computation.1 | async-start | bytes 2228224 | tf_op jit(solution)/shard_map/all_to_all | solution.py:257
  32.4 13.8 %copy-start.2 = (s32[32]{0:T(128)S(1)}, s32[32]{0:T(128)}, u32[]{:S(2)}) copy-start(s32[32]{0:T(128)} %table_ref.1) | copy-start | bytes 388

commit v3 on v2

--- a/solution.py
+++ b/solution.py
@@ -17,6 +17,8 @@
 CHUNKS = BS // LANES
 BODY = CHUNKS * SLOTS * ROWS
 EXTRA = 16
+ORDER = [10, 11, 12, 13, 14, 15, 0, 1, 2, 3, 4, 5, 6, 7, 8, 9]
+CHUNK = [ORDER.index(device) for device in range(DEVICES)]
 VMEM_LIMIT = 12 * 1024 * 1024
 GRAD_PARTS = 4
 
@@ -48,7 +50,7 @@
         copies[-1].start()
     table_copy.wait()
     for s in range(DEVICES * SLOTS):
-        slot_ref[table_ref[s]] = s
+        slot_ref[table_ref[s]] = CHUNK[s // SLOTS] * SLOTS + s % SLOTS
     for block in range(2 * COLUMNS):
         if block % blocks == 0:
             copies[block // blocks].wait()
@@ -109,12 +111,16 @@
     return high, middle, rest - middle
 
 
+def whole_block(owned_ref, t):
+    return jnp.concatenate([owned_ref[chunk, t] for chunk in CHUNK], axis=0)
+
+
 def precondition_kernel(owned_ref, lroot_ref, rroot_ref, out_hbm, out_ref, sem):
     gpart = jnp.zeros((1, LANES), jnp.float32)
     ppart = jnp.zeros((1, LANES), jnp.float32)
     copies = []
     for t in range(SLOTS):
-        block = owned_ref[:, t].reshape(BS, BS)
+        block = whole_block(owned_ref, t)
         half = jnp.dot(lroot_ref[t], block, preferred_element_type=jnp.float32)
         half = half.astype(jnp.bfloat16)
         precond = jnp.dot(half, rroot_ref[t], preferred_element_type=jnp.float32)
@@ -123,7 +129,8 @@
             lanes = slice(q * LANES, (q + 1) * LANES)
             piece = precond[:, lanes]
             start = (t * CHUNKS + q) * ROWS
-            out_ref[:, start : start + ROWS, :] = piece.reshape(DEVICES, ROWS, LANES)
+            for device, chunk in enumerate(CHUNK):
+                out_ref[chunk, start : start + ROWS, :] = piece[device * ROWS : (device + 1) * ROWS]
             pfloat = piece.astype(jnp.float32)
             ppart += jnp.sum(pfloat * pfloat, axis=0, keepdims=True)
             gfloat = block[:, lanes].astype(jnp.float32)
@@ -183,7 +190,7 @@
     weight = (1.0 - stat_decay) / BS
     stores = []
     for t in range(SLOTS):
-        block = owned_ref[:, t].reshape(BS, BS)
+        block = whole_block(owned_ref, t)
         for side, out_hbm in enumerate((left_out, right_out)):
             dims = (((1 - side,), (1 - side,)), ((), ()))
             gram = lax.dot_general(block, block, dims, preferred_element_type=jnp.float32)
@@ -225,7 +232,7 @@
     for s in range(DEVICES * SLOTS):
         for q in range(CHUNKS):
             start = (s % SLOTS * CHUNKS + q) * ROWS
-            pfloat = back_ref[s // SLOTS, start : start + ROWS, :].astype(jnp.float32)
+            pfloat = back_ref[CHUNK[s // SLOTS], start : start + ROWS, :].astype(jnp.float32)
             scaled_ref[s, :, q * LANES : (q + 1) * LANES] = (ratio * pfloat).astype(jnp.bfloat16)
         row, columns = place(table_ref[s])
         pltpu.make_async_copy(scaled_ref.at[s], out_ref.at[row, :, columns], sem).start()
@@ -250,11 +257,17 @@
     )(table, back)
 
 
+def exchange(chunks):
+    return lax.all_to_all(
+        chunks, "fsdp", split_axis=0, concat_axis=0, axis_index_groups=[ORDER], tiled=True
+    )
+
+
 def on_device(grad, left_stat, right_stat, left_root, right_root, table):
     outgoing, decayed = pack(table, grad, right_stat)
-    owned = lax.all_to_all(outgoing, "fsdp", split_axis=0, concat_axis=0, tiled=True)
+    owned = exchange(outgoing)
     returning = precondition(owned, left_root, right_root)
-    back = lax.all_to_all(returning, "fsdp", split_axis=0, concat_axis=0, tiled=True)
+    back = exchange(returning)
     left_new, right_new = statistics(owned, left_stat, right_stat, decayed)
     update = unpack(table, back)
     return (update, left_new, right_new)

time: 48.1 us -> 43.3 us (0.900)
  waiting for transfers between devices: 9.24 us -> 3.8 us
  starting transfers between devices: 3.71 us -> 7.49 us
  blocking collectives: 19.8 us -> 16.6 us
    all_to_all x1, waiting for transfers between devices: 9.24 us -> 3.8 us  [exchange(): lax.all_to_all(chunks, 'fsdp', split_axis=0, concat_axis=0, axis_index_gr...]
    all_to_all x1, starting transfers between devices: 3.71 us -> 7.49 us  [exchange(): lax.all_to_all(chunks, 'fsdp', split_axis=0, concat_axis=0, axis_index_gr...]
    all_to_all x1, blocking collectives: 19.8 us -> 16.6 us  [exchange(): lax.all_to_all(chunks, 'fsdp', split_axis=0, concat_axis=0, axis_index_gr...]
  transfers between devices with their start and end apart: 1 -> 1, of which waited for: 1 -> 1; matrix products, arithmetic and copies ran while one was open for 0% -> 0% of each run, Pallas kernels for 9% -> 10%
where the time goes in v3:
time: 43.3 us; the launch traced here: 43 us
  blocking collectives  16.6 us (38%)
  Pallas kernels  14.4 us (33%)
  starting transfers between devices  7.49 us (17%)
  waiting for transfers between devices  3.8 us (9%)
  between operations  0.68 us (2%)
    all_to_all x1, blocking collectives, exchange(): lax.all_to_all(chunks, 'fsdp', split_axis=0, concat_axis=0, axis_index_gr...  16.6 us
    all_to_all x1, starting transfers between devices, exchange(): lax.all_to_all(chunks, 'fsdp', split_axis=0, concat_axis=0, axis_index_gr...  7.49 us
    pallas_call x1, Pallas kernels, pack(): pl.pallas_call(pack_kernel, out_shape=[jax.ShapeDtypeStruct((DEVICES, SLO...  6.06 us
    pallas_call x1, Pallas kernels, statistics(): pl.pallas_call(statistics_kernel, out_shape=[jax.ShapeDtypeStruct((SLOTS,...  4.51 us
    all_to_all x1, waiting for transfers between devices, exchange(): lax.all_to_all(chunks, 'fsdp', split_axis=0, concat_axis=0, axis_index_gr...  3.8 us
    pallas_call x1, Pallas kernels, precondition(): pl.pallas_call(precondition_kernel, out_shape=jax.ShapeDtypeStruct(shape,...  2.16 us
    pallas_call x1, Pallas kernels, unpack(): pl.pallas_call(unpack_kernel, out_shape=jax.ShapeDtypeStruct((2, ROWS, CO...  1.64 us
  transfers between devices with their start and end apart: 1, of which 1 were waited for; matrix products, arithmetic and copies ran while one was open for 0% of the time, Pallas kernels for 10%

profile of v3, /device:TPU:96, one launch (start us, length us, event | category | flops | bytes accessed | tf_op | source)
XLA Modules:
  0.0 43.0 jit_solution(7578369720062536484)
XLA Ops:
  0.6 0.0 copy-start.1
  0.6 0.0 copy-start
  0.7 6.1 %pack.1 = (bf16[16,2,32,512]{3,2,1,0:T(8,128)(2,1)S(1)}, f32[2,512,512]{2,1,0:T(8,128)}) custom-call(s32[32]{0:T(128)} %table_ref.1, bf16[2,32,8192]{2,1,0:T(8,128)(2,1)} %grad_hbm.1, f32[2,512,512]{2,1,0:T(8,128)} %right_hbm.3), custom_call_target="tpu_custom_call" | custom-call | tf_op jit(solution)/shard_map/pack/pallas_call | solution.py:80
  6.7 16.6 %all_to_all.10.owned_ref = bf16[16,2,32,512]{3,2,1,0:T(8,128)(2,1)S(1)} all-to-all(bf16[16,2,32,512]{3,2,1,0:T(8,128)(2,1)S(1)} %get-tuple-element.7), channel_id=1, replica_groups={{10,11,12,13,14,15,0,1,2,3,4,5,6,7,8,9},{26,27,28,29,30,31,16,17,18,19,..., dimensions={0} | all-to-all | bytes 2097152 | tf_op jit(solution)/shard_map/all_to_all | solution.py:261
  23.3 0.0 copy-done.1
  23.3 0.0 copy-done
  23.3 2.2 %precondition.1 = bf16[16,272,128]{2,1,0:T(8,128)(2,1)} custom-call(bf16[16,2,32,512]{3,2,1,0:T(8,128)(2,1)S(1)} %all_to_all.10.owned_ref, bf16[2,512,512]{2,1,0:T(8,128)(2,1)S(1)} %copy-done, bf16[2,512,512]{2,1,0:T(8,128)(2,1)S(1)} %copy-done.1), custom_call_target="tpu_custom_call" | custom-call | flops 1073741824 | bytes 4194304 | tf_op jit(solution)/shard_map/precondition/pallas_call | solution.py:157
  25.5 7.5 %all-to-all-start.1 = ((bf16[16,272,128]{2,1,0:T(8,128)(2,1)}), bf16[16,272,128]{2,1,0:T(8,128)(2,1)S(1)}, u32[]{:S(2)}, u32[]{:S(2)}) async-start(bf16[16,272,128]{2,1,0:T(8,128)(2,1)} %precondition.1), calls=%async_computation.1 | async-start | bytes 2228224 | tf_op jit(solution)/shard_map/all_to_all | solution.py:261
  33.0 0.0 copy-start.2
  33.0 4.5 %statistics.1 = (f32[2,512,512]{2,1,0:T(8,128)}, f32[2,512,512]{2,1,0:T(8,128)}) custom-call(bf16[16,2,32,512]{3,2,1,0:T(8,128)(2,1)S(1)} %all_to_all.10.owned_ref, f32[2,512,512]{2,1,0:T(8,128)} %left_hbm.1, f32[2,512,512]{2,1,0:T(8,128)} %right_hbm.3, f32[2,512,512]{2,1,0:T(8,128)} %get-tuple-element.8.decayed_hbm), custom_call_target="tpu_custom_call" | custom-call | flops 1073741824 | bytes 9437184 | tf_op jit(solution)/shard_map/statistics/pallas_call | solution.py:208
  37.5 3.8 %all-to-all-done.1.back_ref = bf16[16,272,128]{2,1,0:T(8,128)(2,1)S(1)} async-done(((bf16[16,272,128]{2,1,0:T(8,128)(2,1)}), bf16[16,272,128]{2,1,0:T(8,128)(2,1)S(1)}, u32[]{:S(2)}, u32[]{:S(2)}) %all-to-all-start.1) | async-done | bytes 1114144 | tf_op jit(solution)/shard_map/all_to_all | solution.py:261
  41.3 0.0 copy-done.2
  41.3 1.6 %unpack.1 = bf16[2,32,8192]{2,1,0:T(8,128)(2,1)} custom-call(s32[32]{0:T(128)S(1)} %copy-done.2, bf16[16,272,128]{2,1,0:T(8,128)(2,1)S(1)} %all-to-all-done.1.back_ref), custom_call_target="tpu_custom_call" | custom-call | tf_op jit(solution)/shard_map/unpack/pallas_call | solution.py:243
Async XLA Ops:
  0.6 22.7 %copy-start.1 = (bf16[2,512,512]{2,1,0:T(8,128)(2,1)S(1)}, bf16[2,512,512]{2,1,0:T(8,128)(2,1)}, u32[]{:S(2)}) copy-start(bf16[2,512,512]{2,1,0:T(8,128)(2,1)} %rroot_ref.1) | copy-start | bytes 3145732
  0.6 22.7 %copy-start = (bf16[2,512,512]{2,1,0:T(8,128)(2,1)S(1)}, bf16[2,512,512]{2,1,0:T(8,128)(2,1)}, u32[]{:S(2)}) copy-start(bf16[2,512,512]{2,1,0:T(8,128)(2,1)} %lroot_ref.1) | copy-start | bytes 3145732
  25.5 15.8 %all-to-all-start.1 = ((bf16[16,272,128]{2,1,0:T(8,128)(2,1)}), bf16[16,272,128]{2,1,0:T(8,128)(2,1)S(1)}, u32[]{:S(2)}, u32[]{:S(2)}) async-start(bf16[16,272,128]{2,1,0:T(8,128)(2,1)} %precondition.1), calls=%async_computation.1 | async-start | bytes 2228224 | tf_op jit(solution)/shard_map/all_to_all | solution.py:261
  33.0 8.3 %copy-start.2 = (s32[32]{0:T(128)S(1)}, s32[32]{0:T(128)}, u32[]{:S(2)}) copy-start(s32[32]{0:T(128)} %table_ref.1) | copy-start | bytes 388

commit v4 on v3

--- a/solution.py
+++ b/solution.py
@@ -18,9 +18,12 @@
 BODY = CHUNKS * SLOTS * ROWS
 EXTRA = 16
 ORDER = [10, 11, 12, 13, 14, 15, 0, 1, 2, 3, 4, 5, 6, 7, 8, 9]
+ORDER_BACK = [10, 11, 12, 13, 14, 15, 0, 1, 2, 3, 4, 5, 6, 7, 8, 9]
 CHUNK = [ORDER.index(device) for device in range(DEVICES)]
+CHUNK_BACK = [ORDER_BACK.index(device) for device in range(DEVICES)]
 VMEM_LIMIT = 12 * 1024 * 1024
 GRAD_PARTS = 4
+EARLY = 384
 
 
 def place(block):
@@ -63,7 +66,7 @@
     @pl.when(second_turn())
     def _():
         for t in range(SLOTS):
-            load = pltpu.make_async_copy(right_hbm.at[t], stat_ref, load_sem)
+            load = pltpu.make_async_copy(right_hbm.at[t, :EARLY], stat_ref, load_sem)
             load.start()
             load.wait()
             stat_ref[...] = stat_decay * stat_ref[...]
@@ -81,7 +84,7 @@
         pack_kernel,
         out_shape=[
             jax.ShapeDtypeStruct((DEVICES, SLOTS, ROWS, BS), jnp.bfloat16),
-            pltpu.HBM((SLOTS, BS, BS), jnp.float32),
+            pltpu.HBM((SLOTS, EARLY, BS), jnp.float32),
         ],
         in_specs=[pl.BlockSpec(memory_space=pl.ANY)] * 3,
         out_specs=[
@@ -92,7 +95,7 @@
             pltpu.SMEM((DEVICES * SLOTS,), jnp.int32),
             pltpu.SMEM((DEVICES * SLOTS,), jnp.int32),
             pltpu.VMEM((2, ROWS, COLUMNS * BS), jnp.bfloat16),
-            pltpu.VMEM((BS, BS), jnp.float32),
+            pltpu.VMEM((EARLY, BS), jnp.float32),
             pltpu.SemaphoreType.DMA,
             pltpu.SemaphoreType.DMA((GRAD_PARTS,)),
             pltpu.SemaphoreType.DMA,
@@ -129,7 +132,7 @@
             lanes = slice(q * LANES, (q + 1) * LANES)
             piece = precond[:, lanes]
             start = (t * CHUNKS + q) * ROWS
-            for device, chunk in enumerate(CHUNK):
+            for device, chunk in enumerate(CHUNK_BACK):
                 out_ref[chunk, start : start + ROWS, :] = piece[device * ROWS : (device + 1) * ROWS]
             pfloat = piece.astype(jnp.float32)
             ppart += jnp.sum(pfloat * pfloat, axis=0, keepdims=True)
@@ -175,27 +178,33 @@
     owned_ref, left_hbm, right_hbm, decayed_hbm, left_out, right_out, stat_ref, load_sem, store_sem
 ):
     second = second_turn()
+    late = jnp.where(second, 1.0, stat_decay).astype(jnp.float32)
+    weight = (1.0 - stat_decay) / BS
+    top, bottom, whole = pl.ds(0, EARLY), pl.ds(EARLY, BS - EARLY), pl.ds(0, BS)
+    pieces = ((left_hbm, whole, stat_decay),), ((right_hbm, top, late), (right_hbm, bottom, stat_decay))
     loads = {}
     for t in range(SLOTS):
-        for side, stat_hbm in enumerate((left_hbm, right_hbm)):
-            where, sem = stat_ref.at[side, t], load_sem.at[side, t]
-            loads[side, t] = pltpu.make_async_copy(stat_hbm.at[t], where, sem)
-            if side == 0:
-                loads[side, t].start()
-            else:
-                early = pltpu.make_async_copy(decayed_hbm.at[t], where, sem)
-                pl.when(second)(early.start)
-                pl.when(jnp.logical_not(second))(loads[side, t].start)
-    decays = stat_decay, jnp.where(second, 1.0, stat_decay).astype(jnp.float32)
-    weight = (1.0 - stat_decay) / BS
+        for side in range(2):
+            for k, (stat_hbm, rows, _) in enumerate(pieces[side]):
+                where, sem = stat_ref.at[side, t, rows], load_sem.at[side + k, t]
+                load = pltpu.make_async_copy(stat_hbm.at[t, rows], where, sem)
+                loads[side, t, k] = load
+                if rows is top:
+                    decayed = pltpu.make_async_copy(decayed_hbm.at[t], where, sem)
+                    pl.when(second)(decayed.start)
+                    pl.when(jnp.logical_not(second))(load.start)
+                else:
+                    load.start()
     stores = []
     for t in range(SLOTS):
         block = whole_block(owned_ref, t)
         for side, out_hbm in enumerate((left_out, right_out)):
             dims = (((1 - side,), (1 - side,)), ((), ()))
             gram = lax.dot_general(block, block, dims, preferred_element_type=jnp.float32)
-            loads[side, t].wait()
-            stat_ref[side, t] = decays[side] * stat_ref[side, t] + weight * gram
+            for k, (_, rows, decay) in enumerate(pieces[side]):
+                loads[side, t, k].wait()
+                new = gram[rows.start : rows.start + rows.size]
+                stat_ref[side, t, rows] = decay * stat_ref[side, t, rows] + weight * new
             stores.append(
                 pltpu.make_async_copy(stat_ref.at[side, t], out_hbm.at[t], store_sem.at[side, t])
             )
@@ -212,7 +221,7 @@
         out_specs=[pl.BlockSpec(memory_space=pltpu.HBM)] * 2,
         scratch_shapes=[
             pltpu.VMEM((2, SLOTS, BS, BS), jnp.float32),
-            pltpu.SemaphoreType.DMA((2, SLOTS)),
+            pltpu.SemaphoreType.DMA((3, SLOTS)),
             pltpu.SemaphoreType.DMA((2, SLOTS)),
         ],
         compiler_params=pltpu.CompilerParams(vmem_limit_bytes=VMEM_LIMIT),
@@ -232,7 +241,7 @@
     for s in range(DEVICES * SLOTS):
         for q in range(CHUNKS):
             start = (s % SLOTS * CHUNKS + q) * ROWS
-            pfloat = back_ref[CHUNK[s // SLOTS], start : start + ROWS, :].astype(jnp.float32)
+            pfloat = back_ref[CHUNK_BACK[s // SLOTS], start : start + ROWS, :].astype(jnp.float32)
             scaled_ref[s, :, q * LANES : (q + 1) * LANES] = (ratio * pfloat).astype(jnp.bfloat16)
         row, columns = place(table_ref[s])
         pltpu.make_async_copy(scaled_ref.at[s], out_ref.at[row, :, columns], sem).start()
@@ -257,17 +266,17 @@
     )(table, back)
 
 
-def exchange(chunks):
+def exchange(chunks, order):
     return lax.all_to_all(
-        chunks, "fsdp", split_axis=0, concat_axis=0, axis_index_groups=[ORDER], tiled=True
+        chunks, "fsdp", split_axis=0, concat_axis=0, axis_index_groups=[order], tiled=True
     )
 
 
 def on_device(grad, left_stat, right_stat, left_root, right_root, table):
     outgoing, decayed = pack(table, grad, right_stat)
-    owned = exchange(outgoing)
+    owned = exchange(outgoing, ORDER)
     returning = precondition(owned, left_root, right_root)
-    back = exchange(returning)
+    back = exchange(returning, ORDER_BACK)
     left_new, right_new = statistics(owned, left_stat, right_stat, decayed)
     update = unpack(table, back)
     return (update, left_new, right_new)

time: 43.3 us -> 42.9 us (level)
  Pallas kernels: 14.4 us -> 13.9 us
    pallas_call x1, Pallas kernels: 6.06 us -> 5.61 us  [pack(): pl.pallas_call(pack_kernel, out_shape=[jax.ShapeDtypeStruct((DEVICES, SLO...]
  transfers between devices with their start and end apart: 1 -> 1, of which waited for: 1 -> 1; matrix products, arithmetic and copies ran while one was open for 0% -> 0% of each run, Pallas kernels for 10% -> 11%
where the time goes in v4:
time: 42.9 us; the launch traced here: 42.6 us
  blocking collectives  16.7 us (39%)
  Pallas kernels  13.9 us (32%)
  starting transfers between devices  7.54 us (18%)
  waiting for transfers between devices  3.83 us (9%)
  between operations  0.68 us (2%)
    all_to_all x1, blocking collectives, exchange(): lax.all_to_all(chunks, 'fsdp', split_axis=0, concat_axis=0, axis_index_gr...  16.7 us
    all_to_all x1, starting transfers between devices, exchange(): lax.all_to_all(chunks, 'fsdp', split_axis=0, concat_axis=0, axis_index_gr...  7.54 us
    pallas_call x1, Pallas kernels, pack(): pl.pallas_call(pack_kernel, out_shape=[jax.ShapeDtypeStruct((DEVICES, SLO...  5.61 us
    pallas_call x1, Pallas kernels, statistics(): pl.pallas_call(statistics_kernel, out_shape=[jax.ShapeDtypeStruct((SLOTS,...  4.48 us
    all_to_all x1, waiting for transfers between devices, exchange(): lax.all_to_all(chunks, 'fsdp', split_axis=0, concat_axis=0, axis_index_gr...  3.83 us
    pallas_call x1, Pallas kernels, precondition(): pl.pallas_call(precondition_kernel, out_shape=jax.ShapeDtypeStruct(shape,...  2.16 us
    pallas_call x1, Pallas kernels, unpack(): pl.pallas_call(unpack_kernel, out_shape=jax.ShapeDtypeStruct((2, ROWS, CO...  1.64 us
  transfers between devices with their start and end apart: 1, of which 1 were waited for; matrix products, arithmetic and copies ran while one was open for 0% of the time, Pallas kernels for 11%

profile of v4, /device:TPU:96, one launch (start us, length us, event | category | flops | bytes accessed | tf_op | source)
XLA Modules:
  0.0 42.6 jit_solution(10943769150819370588)
XLA Ops:
  0.6 0.0 copy-start.1
  0.6 0.0 copy-start
  0.7 5.6 %pack.1 = (bf16[16,2,32,512]{3,2,1,0:T(8,128)(2,1)S(1)}, f32[2,384,512]{2,1,0:T(8,128)}) custom-call(s32[32]{0:T(128)} %table_ref.1, bf16[2,32,8192]{2,1,0:T(8,128)(2,1)} %grad_hbm.1, f32[2,512,512]{2,1,0:T(8,128)} %right_hbm.3), custom_call_target="tpu_custom_call" | custom-call | tf_op jit(solution)/shard_map/pack/pallas_call | solution.py:83
  6.3 16.7 %all_to_all.10.owned_ref = bf16[16,2,32,512]{3,2,1,0:T(8,128)(2,1)S(1)} all-to-all(bf16[16,2,32,512]{3,2,1,0:T(8,128)(2,1)S(1)} %get-tuple-element.7), channel_id=1, replica_groups={{10,11,12,13,14,15,0,1,2,3,4,5,6,7,8,9},{26,27,28,29,30,31,16,17,18,19,..., dimensions={0} | all-to-all | bytes 2097152 | tf_op jit(solution)/shard_map/all_to_all | solution.py:270
  23.0 0.0 copy-done.1
  23.0 0.0 copy-done
  23.0 2.2 %precondition.1 = bf16[16,272,128]{2,1,0:T(8,128)(2,1)} custom-call(bf16[16,2,32,512]{3,2,1,0:T(8,128)(2,1)S(1)} %all_to_all.10.owned_ref, bf16[2,512,512]{2,1,0:T(8,128)(2,1)S(1)} %copy-done, bf16[2,512,512]{2,1,0:T(8,128)(2,1)S(1)} %copy-done.1), custom_call_target="tpu_custom_call" | custom-call | flops 1073741824 | bytes 4194304 | tf_op jit(solution)/shard_map/precondition/pallas_call | solution.py:160
  25.1 7.5 %all-to-all-start.1 = ((bf16[16,272,128]{2,1,0:T(8,128)(2,1)}), bf16[16,272,128]{2,1,0:T(8,128)(2,1)S(1)}, u32[]{:S(2)}, u32[]{:S(2)}) async-start(bf16[16,272,128]{2,1,0:T(8,128)(2,1)} %precondition.1), calls=%async_computation.1 | async-start | bytes 2228224 | tf_op jit(solution)/shard_map/all_to_all | solution.py:270
  32.7 0.0 copy-start.2
  32.7 4.5 %statistics.1 = (f32[2,512,512]{2,1,0:T(8,128)}, f32[2,512,512]{2,1,0:T(8,128)}) custom-call(bf16[16,2,32,512]{3,2,1,0:T(8,128)(2,1)S(1)} %all_to_all.10.owned_ref, f32[2,512,512]{2,1,0:T(8,128)} %left_hbm.1, f32[2,512,512]{2,1,0:T(8,128)} %right_hbm.3, f32[2,384,512]{2,1,0:T(8,128)} %get-tuple-element.8.decayed_hbm), custom_call_target="tpu_custom_call" | custom-call | flops 1073741824 | bytes 9437184 | tf_op jit(solution)/shard_map/statistics/pallas_call | solution.py:217
  37.2 3.8 %all-to-all-done.1.back_ref = bf16[16,272,128]{2,1,0:T(8,128)(2,1)S(1)} async-done(((bf16[16,272,128]{2,1,0:T(8,128)(2,1)}), bf16[16,272,128]{2,1,0:T(8,128)(2,1)S(1)}, u32[]{:S(2)}, u32[]{:S(2)}) %all-to-all-start.1) | async-done | bytes 1114144 | tf_op jit(solution)/shard_map/all_to_all | solution.py:270
  41.0 0.0 copy-done.2
  41.0 1.6 %unpack.1 = bf16[2,32,8192]{2,1,0:T(8,128)(2,1)} custom-call(s32[32]{0:T(128)S(1)} %copy-done.2, bf16[16,272,128]{2,1,0:T(8,128)(2,1)S(1)} %all-to-all-done.1.back_ref), custom_call_target="tpu_custom_call" | custom-call | tf_op jit(solution)/shard_map/unpack/pallas_call | solution.py:252
Async XLA Ops:
  0.6 22.3 %copy-start.1 = (bf16[2,512,512]{2,1,0:T(8,128)(2,1)S(1)}, bf16[2,512,512]{2,1,0:T(8,128)(2,1)}, u32[]{:S(2)}) copy-start(bf16[2,512,512]{2,1,0:T(8,128)(2,1)} %rroot_ref.1) | copy-start | bytes 3145732
  0.6 22.3 %copy-start = (bf16[2,512,512]{2,1,0:T(8,128)(2,1)S(1)}, bf16[2,512,512]{2,1,0:T(8,128)(2,1)}, u32[]{:S(2)}) copy-start(bf16[2,512,512]{2,1,0:T(8,128)(2,1)} %lroot_ref.1) | copy-start | bytes 3145732
  25.1 15.9 %all-to-all-start.1 = ((bf16[16,272,128]{2,1,0:T(8,128)(2,1)}), bf16[16,272,128]{2,1,0:T(8,128)(2,1)S(1)}, u32[]{:S(2)}, u32[]{:S(2)}) async-start(bf16[16,272,128]{2,1,0:T(8,128)(2,1)} %precondition.1), calls=%async_computation.1 | async-start | bytes 2228224 | tf_op jit(solution)/shard_map/all_to_all | solution.py:270
  32.7 8.3 %copy-start.2 = (s32[32]{0:T(128)S(1)}, s32[32]{0:T(128)}, u32[]{:S(2)}) copy-start(s32[32]{0:T(128)} %table_ref.1) | copy-start | bytes 388

commit v5 on v4

--- a/solution.py
+++ b/solution.py
@@ -102,6 +102,11 @@
             pltpu.SemaphoreType.DMA,
         ],
         compiler_params=pltpu.CompilerParams(vmem_limit_bytes=VMEM_LIMIT),
+        cost_estimate=pl.CostEstimate(
+            flops=SLOTS * EARLY * BS,
+            bytes_accessed=4 * DEVICES * SLOTS * ROWS * BS + 8 * SLOTS * EARLY * BS,
+            transcendentals=0,
+        ),
         name="pack",
     )(*map(in_hbm, (table, grad, right_stat)))
 

time: 42.9 us -> 42.9 us (level)
  no operation moved by 1% of the time
where the time goes in v5:
time: 42.9 us; the launch traced here: 42.6 us
  blocking collectives  16.7 us (39%)
  Pallas kernels  13.9 us (32%)
  starting transfers between devices  7.54 us (18%)
  waiting for transfers between devices  3.83 us (9%)
  between operations  0.68 us (2%)
    all_to_all x1, blocking collectives, exchange(): lax.all_to_all(chunks, 'fsdp', split_axis=0, concat_axis=0, axis_index_gr...  16.7 us
    all_to_all x1, starting transfers between devices, exchange(): lax.all_to_all(chunks, 'fsdp', split_axis=0, concat_axis=0, axis_index_gr...  7.54 us
    pallas_call x1, Pallas kernels, pack(): pl.pallas_call(pack_kernel, out_shape=[jax.ShapeDtypeStruct((DEVICES, SLO...  5.61 us
    pallas_call x1, Pallas kernels, statistics(): pl.pallas_call(statistics_kernel, out_shape=[jax.ShapeDtypeStruct((SLOTS,...  4.48 us
    all_to_all x1, waiting for transfers between devices, exchange(): lax.all_to_all(chunks, 'fsdp', split_axis=0, concat_axis=0, axis_index_gr...  3.83 us
    pallas_call x1, Pallas kernels, precondition(): pl.pallas_call(precondition_kernel, out_shape=jax.ShapeDtypeStruct(shape,...  2.16 us
    pallas_call x1, Pallas kernels, unpack(): pl.pallas_call(unpack_kernel, out_shape=jax.ShapeDtypeStruct((2, ROWS, CO...  1.64 us
  transfers between devices with their start and end apart: 1, of which 1 were waited for; matrix products, arithmetic and copies ran while one was open for 0% of the time, Pallas kernels for 11%

profile of v5, /device:TPU:96, one launch (start us, length us, event | category | flops | bytes accessed | tf_op | source)
XLA Modules:
  0.0 42.6 jit_solution(10943769150819370588)
XLA Ops:
  0.6 0.0 copy-start.1
  0.6 0.0 copy-start
  0.7 5.6 %pack.1 = (bf16[16,2,32,512]{3,2,1,0:T(8,128)(2,1)S(1)}, f32[2,384,512]{2,1,0:T(8,128)}) custom-call(s32[32]{0:T(128)} %table_ref.1, bf16[2,32,8192]{2,1,0:T(8,128)(2,1)} %grad_hbm.1, f32[2,512,512]{2,1,0:T(8,128)} %right_hbm.3), custom_call_target="tpu_custom_call" | custom-call | flops 393216 | bytes 5242880 | tf_op jit(solution)/shard_map/pack/pallas_call | solution.py:83
  6.3 16.7 %all_to_all.10.owned_ref = bf16[16,2,32,512]{3,2,1,0:T(8,128)(2,1)S(1)} all-to-all(bf16[16,2,32,512]{3,2,1,0:T(8,128)(2,1)S(1)} %get-tuple-element.7), channel_id=1, replica_groups={{10,11,12,13,14,15,0,1,2,3,4,5,6,7,8,9},{26,27,28,29,30,31,16,17,18,19,..., dimensions={0} | all-to-all | bytes 2097152 | tf_op jit(solution)/shard_map/all_to_all | solution.py:275
  23.0 0.0 copy-done.1
  23.0 0.0 copy-done
  23.0 2.2 %precondition.1 = bf16[16,272,128]{2,1,0:T(8,128)(2,1)} custom-call(bf16[16,2,32,512]{3,2,1,0:T(8,128)(2,1)S(1)} %all_to_all.10.owned_ref, bf16[2,512,512]{2,1,0:T(8,128)(2,1)S(1)} %copy-done, bf16[2,512,512]{2,1,0:T(8,128)(2,1)S(1)} %copy-done.1), custom_call_target="tpu_custom_call" | custom-call | flops 1073741824 | bytes 4194304 | tf_op jit(solution)/shard_map/precondition/pallas_call | solution.py:165
  25.1 7.5 %all-to-all-start.1 = ((bf16[16,272,128]{2,1,0:T(8,128)(2,1)}), bf16[16,272,128]{2,1,0:T(8,128)(2,1)S(1)}, u32[]{:S(2)}, u32[]{:S(2)}) async-start(bf16[16,272,128]{2,1,0:T(8,128)(2,1)} %precondition.1), calls=%async_computation.1 | async-start | bytes 2228224 | tf_op jit(solution)/shard_map/all_to_all | solution.py:275
  32.7 0.0 copy-start.2
  32.7 4.5 %statistics.1 = (f32[2,512,512]{2,1,0:T(8,128)}, f32[2,512,512]{2,1,0:T(8,128)}) custom-call(bf16[16,2,32,512]{3,2,1,0:T(8,128)(2,1)S(1)} %all_to_all.10.owned_ref, f32[2,512,512]{2,1,0:T(8,128)} %left_hbm.1, f32[2,512,512]{2,1,0:T(8,128)} %right_hbm.3, f32[2,384,512]{2,1,0:T(8,128)} %get-tuple-element.8.decayed_hbm), custom_call_target="tpu_custom_call" | custom-call | flops 1073741824 | bytes 9437184 | tf_op jit(solution)/shard_map/statistics/pallas_call | solution.py:222
  37.2 3.8 %all-to-all-done.1.back_ref = bf16[16,272,128]{2,1,0:T(8,128)(2,1)S(1)} async-done(((bf16[16,272,128]{2,1,0:T(8,128)(2,1)}), bf16[16,272,128]{2,1,0:T(8,128)(2,1)S(1)}, u32[]{:S(2)}, u32[]{:S(2)}) %all-to-all-start.1) | async-done | bytes 1114144 | tf_op jit(solution)/shard_map/all_to_all | solution.py:275
  41.0 0.0 copy-done.2
  41.0 1.6 %unpack.1 = bf16[2,32,8192]{2,1,0:T(8,128)(2,1)} custom-call(s32[32]{0:T(128)S(1)} %copy-done.2, bf16[16,272,128]{2,1,0:T(8,128)(2,1)S(1)} %all-to-all-done.1.back_ref), custom_call_target="tpu_custom_call" | custom-call | tf_op jit(solution)/shard_map/unpack/pallas_call | solution.py:257
Async XLA Ops:
  0.6 22.3 %copy-start.1 = (bf16[2,512,512]{2,1,0:T(8,128)(2,1)S(1)}, bf16[2,512,512]{2,1,0:T(8,128)(2,1)}, u32[]{:S(2)}) copy-start(bf16[2,512,512]{2,1,0:T(8,128)(2,1)} %rroot_ref.1) | copy-start | bytes 3145732
  0.6 22.3 %copy-start = (bf16[2,512,512]{2,1,0:T(8,128)(2,1)S(1)}, bf16[2,512,512]{2,1,0:T(8,128)(2,1)}, u32[]{:S(2)}) copy-start(bf16[2,512,512]{2,1,0:T(8,128)(2,1)} %lroot_ref.1) | copy-start | bytes 3145732
  25.1 15.9 %all-to-all-start.1 = ((bf16[16,272,128]{2,1,0:T(8,128)(2,1)}), bf16[16,272,128]{2,1,0:T(8,128)(2,1)S(1)}, u32[]{:S(2)}, u32[]{:S(2)}) async-start(bf16[16,272,128]{2,1,0:T(8,128)(2,1)} %precondition.1), calls=%async_computation.1 | async-start | bytes 2228224 | tf_op jit(solution)/shard_map/all_to_all | solution.py:275
  32.7 8.3 %copy-start.2 = (s32[32]{0:T(128)S(1)}, s32[32]{0:T(128)}, u32[]{:S(2)}) copy-start(s32[32]{0:T(128)} %table_ref.1) | copy-start | bytes 388
